TPU v7x, 32 devices: a whole 2x2x4 slice. The times are simulated.
32 devices in a mesh: group: 2 (over x), blk: 16 (over z, y, core).
Axes of the slice: x: 2, y: 2, z: 4, core: 2. Of those that a mesh axis runs over, the one named last changes fastest.
Arguments:
- wavefunction: bfloat16 [256, 3, 128, 128], P(('group', 'blk')), parts along dimension 0, may hold values from -6 to 6
- left_operators: bfloat16 [256, 16, 128, 128], P(('group', 'blk')), parts along dimension 0, may hold values from -0.5 to 0.5
- right_operators: bfloat16 [4096, 128, 128], P(('group', 'blk')), parts along dimension 0, may hold values from -0.5 to 0.5
- shifts: int32 [32], P('group'), parts along dimension 0, may hold values from -1 to 1
- term_mask: int32 [256, 16], P(('group', 'blk')), parts along dimension 0, may hold values 0 or 1
- slot_table: int32 [256, 16], P(('group', 'blk')), parts along dimension 0, may hold values from 0 to 127, as said below
Outputs:
- product_vectors: bfloat16 [256, 3, 128, 128], P(('group', 'blk')), parts along dimension 0
There are 2 independent parts, one for each index of `group`. A program takes and returns all parts, laid end to end along the dimension named above; each array names one. Nothing has to cross between parts.
Inputs may be any that keep to these rules, and one draw needn't show every extreme that they name: `slot_table`: for the 8 blocks of one device, the 128 entries are a permutation of 0 to 127, so every device owns exactly 8 right operator for each device's blocks.
All inputs are finite; a program needn't handle non-finite values. No bound on the sum of `term_mask` on one device may be relied on, other than what follows from the above.
Results may differ from a plain program's by a relative error of at most 0.008.
Values may be sent and summed in bfloat16 or wider, within the bound.
A program may use at most 128 MiB of HBM per device.

v0:
```python
import jax
import jax.numpy as jnp
from jax import lax
from jax.sharding import PartitionSpec as P


def padded(cells, sides, width):
    for axis, dim in sides:
        count = lax.axis_size(axis)
        ends = count - 1
        head = lax.slice_in_dim(cells, 0, width, axis=dim)
        tail = lax.slice_in_dim(cells, cells.shape[dim] - width, cells.shape[dim], axis=dim)
        cells = jnp.concatenate(
            [
                lax.ppermute(tail, axis, [(i, (i + 1) % count) for i in range(ends)]),
                cells,
                lax.ppermute(head, axis, [((i + 1) % count, i) for i in range(ends)]),
            ],
            axis=dim,
        )
    return cells


def per_device(wavefunction, left_operators, right_operators, shifts, term_mask, slot_table):
    blocks = wavefunction.shape[0]
    term_count = left_operators.shape[1]
    vectors = wavefunction.shape[1]
    width = wavefunction.shape[2]
    rimmed = padded(wavefunction, (("blk", 0),), 1)
    before = rimmed[0:blocks]
    middle = rimmed[1 : blocks + 1]
    later_block = rimmed[2 : blocks + 2]
    shift_col = shifts[:, None, None, None, None]
    chosen = jnp.where(
        shift_col == 1, before[None], jnp.where(shift_col == 0, middle[None], later_block[None])
    )
    products = jnp.einsum(
        "itxy,tivyz->itvxz", left_operators, chosen, preferred_element_type=jnp.float32
    )
    weights = term_mask.astype(jnp.float32)[:, :, None, None, None]
    left_done = (products * weights).astype(jnp.bfloat16)
    devices = lax.axis_size("blk")
    item_count = blocks * term_count
    per_peer = item_count // devices
    flat_slot = slot_table.reshape(item_count)
    positions = jnp.arange(item_count, dtype=jnp.int32)
    inverse = jnp.sum(
        jnp.where(flat_slot[None, :] == positions[:, None], positions[None, :], 0), axis=1
    )
    left_items = left_done.reshape(item_count, vectors, width, width)
    outgoing = jnp.take(left_items, inverse, axis=0).reshape(
        devices, per_peer, vectors, width, width
    )
    arrived = lax.all_to_all(outgoing, "blk", split_axis=0, concat_axis=0, tiled=True)
    local_right = right_operators.reshape(devices, per_peer, width, width)
    partial_value = jnp.einsum(
        "spvxy,spzy->spvxz", arrived, local_right, preferred_element_type=jnp.float32
    ).astype(jnp.bfloat16)
    returned = lax.all_to_all(partial_value, "blk", split_axis=0, concat_axis=0, tiled=True)
    terms_done = jnp.take(returned.reshape(item_count, vectors, width, width), flat_slot, axis=0)
    grouped = terms_done.reshape(blocks, term_count, vectors, width, width).astype(jnp.float32)
    return jnp.sum(grouped, axis=1).astype(jnp.bfloat16)


def solution(mesh):
    placed = (
        P(("group", "blk"), None, None, None),
        P(("group", "blk"), None, None, None),
        P(("group", "blk"), None, None),
        P("group"),
        P(("group", "blk"), None),
        P(("group", "blk"), None),
    )
    return jax.shard_map(
        per_device,
        mesh=mesh,
        in_specs=placed,
        out_specs=P(("group", "blk"), None, None, None),
        check_vma=False,
    )
```

profile of v0, /device:TPU:13, one launch (start us, length us, event | category | flops | bytes accessed | tf_op | source)
XLA Modules:
  0.0 653.1 jit_solution(6281213680339270064)
XLA Ops:
  0.0 1.0 fusion.11
  1.0 3.7 collective-permute-start
  4.7 1.9 collective-permute-start.1
  6.6 1.5 copy.12
  8.1 0.8 eq.25
  8.9 0.1 select_reduce_fusion
  9.0 0.7 broadcast_compare_fusion.1
  9.7 0.7 convert_element_type.14
  10.4 0.0 collective-permute-done
  10.4 1.1 collective-permute-done.1
  11.5 1.5 pad_maximum_fusion.1
  13.0 0.4 copy.11
  13.4 0.4 copy.13
  13.7 10.5 %multiply_convert_fusion = bf16[8,16,3,128,128]{4,3,2,1,0:T(8,128)(2,1)} fusion(f32[8,16]{1,0:T(8,128)S(1)} %convert_element_type.14, pred[16]{0:T(512)(128)(4,1)S(1)} %get-tuple-element.11, pred[16]{0:T(512)(128)(4,1)S(1)} %get-tuple-element.10, bf16[8,3,128,128]{2,3,1,0:T(8,128)(2,1)S(1)} %copy.13, bf16[8,3,128,128]{2,3,1,0:T(8,128)(2,1)S(1)} %copy.12, ...), kind=kOutput, calls=%fused_computation.2 | convolution fusion | flops 1635778560 | bytes 19137056 | tf_op jit(solution)/shard_map/itxy,tivyz->itvxz/dot_general | solution.py:37
  24.3 13.0 %gather_fusion = bf16[128,3,128,128]{2,3,1,0:T(8,128)(2,1)} fusion(bf16[128,3,128,128]{2,3,1,0:T(8,128)(2,1)} %bitcast.20, s32[1024]{0:T(1024)S(1)} %pad_clamp_fusion.1), kind=kCustom, calls=%fused_computation.clone | custom fusion | bytes 25166336 | tf_op jit(solution)/shard_map/jit(_take)/gather | solution.py:51
  37.3 11.2 %broadcast_select_fusion.1 = bf16[128,3,128,128]{2,3,1,0:T(8,128)(2,1)} fusion(bf16[128,3,128,128]{2,3,1,0:T(8,128)(2,1)} %gather_fusion, pred[128]{0:T(512)(128)(4,1)S(1)} %compare_and_fusion.1), kind=kLoop, calls=%fused_computation.8 | loop fusion | flops 6291456 | bytes 25165952 | tf_op jit(solution)/shard_map/jit(_take)/select_n | solution.py:51
  48.4 16.6 %copy.14 = bf16[128,3,128,128]{3,2,1,0:T(8,128)(2,1)} copy(bf16[128,3,128,128]{2,3,1,0:T(8,128)(2,1)} %broadcast_select_fusion.1) | data formatting | bytes 25165824 | tf_op jit(solution)/shard_map/jit(_take)/select_n | solution.py:51
  65.1 0.0 copy-start
  65.1 277.9 %all_to_all.10 = bf16[16,8,3,128,128]{4,3,2,1,0:T(8,128)(2,1)} all-to-all(bf16[16,8,3,128,128]{4,3,2,1,0:T(8,128)(2,1)} %bitcast.19), channel_id=1, replica_groups=mesh['group'=2,'blk'=16] {'blk'}, dimensions={0} | all-to-all | bytes 25165824 | tf_op jit(solution)/shard_map/all_to_all | solution.py:54
  343.0 0.0 copy-done
  343.0 9.1 %convolution_convert_fusion = bf16[16,8,3,128,128]{4,3,2,1,0:T(8,128)(2,1)} fusion(bf16[16,8,3,128,128]{4,3,2,1,0:T(8,128)(2,1)} %all_to_all.10, bf16[16,8,128,128,1]{3,2,4,1,0:T(8,128)(2,1)S(1)} %bitcast.21), kind=kOutput, calls=%fused_computation.11 | convolution fusion | flops 1616904192 | bytes 29360128 | tf_op jit(solution)/shard_map/spvxy,spzy->spvxz/dot_general | solution.py:56
  352.1 6.0 all-to-all-start.1
  358.1 272.2 %all-to-all-done.1 = bf16[16,8,3,128,128]{4,3,2,1,0:T(8,128)(2,1)} async-done(((bf16[16,8,3,128,128]{4,3,2,1,0:T(8,128)(2,1)}), bf16[16,8,3,128,128]{4,3,2,1,0:T(8,128)(2,1)}, u32[]{:S(2)}, u32[]{:S(2)}) %all-to-all-start.1) | async-done | bytes 12582944 | tf_op jit(solution)/shard_map/all_to_all | solution.py:59
  630.3 12.9 %gather_fusion.1 = bf16[128,3,128,128]{3,2,1,0:T(8,128)(2,1)} fusion(bf16[128,3,128,128]{3,2,1,0:T(8,128)(2,1)} %bitcast.8, s32[1024]{0:T(1024)S(1)} %pad_clamp_fusion), kind=kCustom, calls=%fused_computation.1.clone | custom fusion | bytes 25166336 | tf_op jit(solution)/shard_map/jit(_take)/gather | solution.py:60
  643.2 9.9 %bitcast_reduce_fusion = bf16[8,3,128,128]{3,2,1,0:T(8,128)(2,1)} fusion(bf16[128,3,128,128]{3,2,1,0:T(8,128)(2,1)} %gather_fusion.1, pred[128]{0:T(512)(128)(4,1)S(1)} %compare_and_fusion), kind=kLoop, calls=%fused_computation.3 | loop fusion | flops 12189696 | bytes 13369472 | tf_op jit(solution)/shard_map/reduce_sum | solution.py:62
  (6 shorter events, 0.0 us)
Async XLA Ops:
  1.0 9.4 %collective-permute-start = (bf16[1,3,128,128]{3,2,1,0:T(8,128)(2,1)S(1)}, bf16[1,3,128,128]{3,2,1,0:T(8,128)(2,1)S(1)}, u32[]{:S(2)}, u32[]{:S(2)}) collective-permute-start(bf16[1,3,128,128]{3,2,1,0:T(8,128)(2,1)S(1)} %get-tuple-element.8), channel_id=1, source_target_pairs={{0,1},{1,2},{2,3},{3,4},{4,5},{5,6},{6,7},{7,8},{8,9},{9,10},{10,1... | collective-permute-start | bytes 294920 | tf_op jit(solution)/shard_map/ppermute | solution.py:15
  4.7 6.8 %collective-permute-start.1 = (bf16[1,3,128,128]{3,2,1,0:T(8,128)(2,1)S(1)}, bf16[1,3,128,128]{3,2,1,0:T(8,128)(2,1)S(1)}, u32[]{:S(2)}, u32[]{:S(2)}) collective-permute-start(bf16[1,3,128,128]{3,2,1,0:T(8,128)(2,1)S(1)} %get-tuple-element.9), channel_id=1, source_target_pairs={{1,0},{2,1},{3,2},{4,3},{5,4},{6,5},{7,6},{8,7},{9,8},{10,9},{11,1... | collective-permute-start | bytes 294920 | tf_op jit(solution)/shard_map/ppermute | solution.py:17
  65.1 277.9 %copy-start = (bf16[128,128,128]{2,1,0:T(8,128)(2,1)S(1)}, bf16[128,128,128]{2,1,0:T(8,128)(2,1)}, u32[]{:S(2)}) copy-start(bf16[128,128,128]{2,1,0:T(8,128)(2,1)} %param.10) | copy-start | bytes 12582916
  352.1 278.2 %all-to-all-start.1 = ((bf16[16,8,3,128,128]{4,3,2,1,0:T(8,128)(2,1)}), bf16[16,8,3,128,128]{4,3,2,1,0:T(8,128)(2,1)}, u32[]{:S(2)}, u32[]{:S(2)}) async-start(bf16[16,8,3,128,128]{4,3,2,1,0:T(8,128)(2,1)} %convolution_convert_fusion), calls=%async_computation.1 | async-start | bytes 25165824 | tf_op jit(solution)/shard_map/all_to_all | solution.py:59
where the time goes:
time: 654 us; the launch traced here: 653 us
  blocking collectives  278 us (43%)
  waiting for transfers between devices  273 us (42%)
  local copies, waits for them, and re-layouts  46.6 us (7%)
  other arithmetic  24 us (4%)
  matrix products  19.6 us (3%)
  starting transfers between devices  11.6 us (2%)
    all_to_all x1, blocking collectives, per_device(): lax.all_to_all(outgoing, 'blk', split_axis=0, concat_axis=0, tiled=True)  278 us
    all_to_all x1, waiting for transfers between devices, per_device(): lax.all_to_all(partial_value, 'blk', split_axis=0, concat_axis=0, tiled=T...  272 us
    select_n x1, local copies, waits for them, and re-layouts, per_device(): jnp.take(left_items, inverse, axis=0)  16.6 us
  transfers between devices with their start and end apart: 3, of which 2 were waited for; matrix products, arithmetic and copies ran while one was open for 1% of the time, Pallas kernels for 0%

commit v1 on v0

v1 whole, which is shorter than its diff:
```python
import functools

import jax
import jax.numpy as jnp
from jax import lax
from jax.experimental import pallas as pl
from jax.experimental.pallas import tpu as pltpu
from jax.sharding import PartitionSpec as P

MESH = pl.DeviceIdType.MESH
PIECES = 1


def partner(me, k, n):
    out = 0
    bit = 1
    while bit < n:
        out = out + bit * ((me // bit + k // bit) % 2)
        bit *= 2
    return out


def offset_of(step, n):
    odd = step % 2
    return (1 - odd) * (n // 2 + step // 2) + odd * ((step + 1) // 2)


def kernel(
    n, pieces, shifts, mask, slots, slots_v, wave, left, right, out,
    wpad, left_v, done, recv, terms, inverse,
    local_sem, left_sem, halo_send, halo_recv, send_sem, recv_sem,
):
    me = lax.axis_index("blk")
    blocks, term_count = left.shape[0], left.shape[1]
    vectors, width = wave.shape[1], wave.shape[2]
    items = blocks * term_count
    per = items // n
    size = per // pieces
    last = n - 1

    barrier = pltpu.get_barrier_semaphore()

    @pl.loop(1, n)
    def _(k):
        pl.semaphore_signal(
            barrier, inc=1, device_id={"blk": partner(me, k, n)}, device_id_type=MESH
        )

    wave_copy = pltpu.make_async_copy(wave, wpad.at[pl.ds(1, blocks)], local_sem.at[0])
    wave_copy.start()
    own = pl.ds(me * per, per)
    own_copy = pltpu.make_async_copy(right.at[own], recv.at[own], local_sem.at[1])
    own_copy.start()
    left_copies = [
        pltpu.make_async_copy(left.at[a], left_v.at[a], left_sem.at[a]) for a in range(blocks)
    ]
    for copy in left_copies:
        copy.start()

    pl.semaphore_wait(barrier, n - 1)

    def halo(up):
        return pltpu.make_async_remote_copy(
            src_ref=wave.at[blocks - 1 if up else 0],
            dst_ref=wpad.at[0 if up else blocks + 1],
            send_sem=halo_send.at[1 if up else 0],
            recv_sem=halo_recv.at[1 if up else 0],
            device_id={"blk": (me + 1) % n if up else (me + n - 1) % n},
            device_id_type=MESH,
        )

    @pl.when(me < last)
    def _():
        halo(True).start()

    @pl.when(me > 0)
    def _():
        halo(False).start()

    def sending(step, piece):
        peer = partner(me, offset_of(step, n), n)
        return pltpu.make_async_remote_copy(
            src_ref=right.at[pl.ds(peer * per + piece * size, size)],
            dst_ref=recv.at[pl.ds(me * per + piece * size, size)],
            send_sem=send_sem.at[piece, step],
            recv_sem=recv_sem.at[piece, step],
            device_id={"blk": peer},
            device_id_type=MESH,
        )

    def arriving(step, piece):
        peer = partner(me, offset_of(step, n), n)
        here = recv.at[pl.ds(peer * per + piece * size, size)]
        return pltpu.make_async_remote_copy(
            src_ref=here,
            dst_ref=here,
            send_sem=send_sem.at[piece, step],
            recv_sem=recv_sem.at[piece, step],
            device_id={"blk": peer},
            device_id_type=MESH,
        )

    for piece in range(pieces):

        @pl.loop(0, n - 1)
        def _(step, piece=piece):
            sending(step, piece).start()

    table = slots_v[...]
    place = lax.broadcasted_iota(jnp.int32, table.shape, 0) * term_count + lax.broadcasted_iota(
        jnp.int32, table.shape, 1
    )

    @pl.loop(0, items)
    def _(s):
        inverse[s] = jnp.max(jnp.where(table == s, place, 0))

    wave_copy.wait()

    @pl.when(me < last)
    def _():
        halo(True).wait_send()
        halo(False).wait_recv()

    @pl.when(me > 0)
    def _():
        halo(False).wait_send()
        halo(True).wait_recv()

    @pl.when(me == 0)
    def _():
        wpad[0] = jnp.zeros(wpad.shape[1:], wpad.dtype)

    @pl.when(me == last)
    def _():
        wpad[blocks + 1] = jnp.zeros(wpad.shape[1:], wpad.dtype)

    for copy in left_copies:
        copy.wait()

    @pl.loop(0, blocks)
    def _(a):
        @pl.loop(0, term_count)
        def _(t):
            row = a + 1 - shifts[t]
            piece = wpad[row]
            beside = jnp.concatenate([piece[v] for v in range(vectors)], axis=1)
            product = jnp.dot(left_v[a, t], beside, preferred_element_type=jnp.float32)
            product = (product * mask[a, t].astype(jnp.float32)).astype(jnp.bfloat16)
            for v in range(vectors):
                done[a * term_count + t, pl.ds(v * width, width)] = product[
                    :, v * width : (v + 1) * width
                ]

    def multiply(first, count):
        for j in range(count):
            s = first + j
            terms[s] = lax.dot_general(
                done[inverse[s]],
                recv[s],
                (((1,), (1,)), ((), ())),
                preferred_element_type=jnp.float32,
            ).astype(jnp.bfloat16)

    own_copy.wait()
    multiply(me * per, per)
    for piece in range(pieces):

        @pl.loop(0, n - 1)
        def _(step, piece=piece):
            arriving(step, piece).wait_recv()
            multiply(partner(me, offset_of(step, n), n) * per + piece * size, size)

    @pl.loop(0, blocks)
    def _(a):
        for v in range(vectors):
            total = jnp.zeros((width, width), jnp.float32)
            for t in range(term_count):
                total += terms[slots[a, t], pl.ds(v * width, width)].astype(jnp.float32)
            out[a, v] = total.astype(out.dtype)

    for piece in range(pieces):

        @pl.loop(0, n - 1)
        def _(step, piece=piece):
            sending(step, piece).wait_send()


def per_device(wavefunction, left_operators, right_operators, shifts, term_mask, slot_table):
    n = lax.axis_size("blk")
    blocks, vectors, width = wavefunction.shape[:3]
    term_count = left_operators.shape[1]
    items = blocks * term_count
    per = items // n
    pieces = PIECES if per % PIECES == 0 else 1
    smem = pl.BlockSpec(memory_space=pltpu.SMEM)
    vmem = pl.BlockSpec(memory_space=pltpu.VMEM)
    hbm = pl.BlockSpec(memory_space=pl.ANY)
    dma = pltpu.SemaphoreType.DMA
    return pl.pallas_call(
        functools.partial(kernel, n, pieces),
        out_shape=jax.ShapeDtypeStruct(wavefunction.shape, jnp.bfloat16),
        in_specs=[smem, smem, smem, vmem, hbm, hbm, hbm],
        out_specs=vmem,
        scratch_shapes=[
            pltpu.VMEM((blocks + 2, vectors, width, width), jnp.bfloat16),
            pltpu.VMEM((blocks, term_count, width, width), jnp.bfloat16),
            pltpu.VMEM((items, vectors * width, width), jnp.bfloat16),
            pltpu.VMEM((items, width, width), jnp.bfloat16),
            pltpu.VMEM((items, vectors * width, width), jnp.bfloat16),
            pltpu.SMEM((items,), jnp.int32),
            dma((2,)),
            dma((blocks,)),
            dma((2,)),
            dma((2,)),
            dma((pieces, n - 1)),
            dma((pieces, n - 1)),
        ],
        compiler_params=pltpu.CompilerParams(
            collective_id=0, has_side_effects=True, vmem_limit_bytes=52 * 1024 * 1024
        ),
        cost_estimate=pl.CostEstimate(
            flops=4 * items * vectors * width**3,
            bytes_accessed=4 * items * width * width,
            transcendentals=0,
        ),
        name="sector_product",
    )(shifts, term_mask, slot_table, slot_table, wavefunction, left_operators, right_operators)


def solution(mesh):
    placed = (
        P(("group", "blk"), None, None, None),
        P(("group", "blk"), None, None, None),
        P(("group", "blk"), None, None),
        P("group"),
        P(("group", "blk"), None),
        P(("group", "blk"), None),
    )
    return jax.shard_map(
        per_device,
        mesh=mesh,
        in_specs=placed,
        out_specs=P(("group", "blk"), None, None, None),
        check_vma=False,
    )
```

time: 654 us -> 104 us (0.16)
  blocking collectives: 278 us -> 0 us
  waiting for transfers between devices: 273 us -> 0 us
  Pallas kernels: 0 us -> 99.8 us
  local copies, waits for them, and re-layouts: 46.6 us -> 4.04 us
  other arithmetic: 24 us -> 0 us
  matrix products: 19.6 us -> 0 us
  starting transfers between devices: 11.6 us -> 0 us
    all_to_all x1 -> x0, blocking collectives: 278 us -> none  [per_device(): lax.all_to_all(outgoing, 'blk', split_axis=0, concat_axis=0, tiled=True)]
    all_to_all x1 -> x0, waiting for transfers between devices: 272 us -> none  [per_device(): lax.all_to_all(partial_value, 'blk', split_axis=0, concat_axis=0, tiled=T...]
    pallas_call x0 -> x1, Pallas kernels: none -> 99.8 us  [per_device(): pl.pallas_call(functools.partial(kernel, n, pieces), out_shape=jax.ShapeD...]
    gather x2 -> x0, local copies, waits for them, and re-layouts: 25.9 us -> none  [the longest x1 13 us: per_device(): jnp.take(left_items, inverse, axis=0)]
    dot_general x2 -> x0, matrix products: 19.6 us -> none  [the longest x1 10.5 us: per_device(): jnp.einsum('itxy,tivyz->itvxz', left_operators, chosen, preferred_element...]
    select_n x1 -> x0, local copies, waits for them, and re-layouts: 16.6 us -> none  [per_device(): jnp.take(left_items, inverse, axis=0)]
    select_n x3 -> x0, other arithmetic: 11.2 us -> none  [the longest x2 11.2 us: per_device(): jnp.take(left_items, inverse, axis=0)]
    reduce_sum x2 -> x0, other arithmetic: 10 us -> none  [the longest x1 9.92 us: per_device(): return jnp.sum(grouped, axis=1).astype(jnp.bfloat16)]
  transfers between devices with their start and end apart: 3 -> 0, of which waited for: 2 -> 0; matrix products, arithmetic and copies ran while one was open for 1% -> 0% of each run, Pallas kernels for 0% -> 0%
where the time goes in v1:
time: 104 us
  Pallas kernels  99.8 us (96%)
  local copies, waits for them, and re-layouts  4.04 us (4%)
    pallas_call x1, Pallas kernels, per_device(): pl.pallas_call(functools.partial(kernel, n, pieces), out_shape=jax.ShapeD...  99.8 us
    unnamed x9, local copies, waits for them, and re-layouts  4.04 us

profile of v1, /device:TPU:13, one launch (start us, length us, event | category | flops | bytes accessed | tf_op | source)
XLA Modules:
  0.0 103.8 jit_solution(1521032411261300769)
XLA Ops:
  0.0 0.0 copy-start
  0.0 1.1 %copy-done = bf16[8,3,128,128]{3,2,1,0:T(8,128)(2,1)S(1)} copy-done((bf16[8,3,128,128]{3,2,1,0:T(8,128)(2,1)S(1)}, bf16[8,3,128,128]{3,2,1,0:T(8,128)(2,1)}, u32[]{:S(2)}) %copy-start) | copy-done | bytes 786456
  1.1 0.0 copy-start.1
  1.1 0.7 copy-done.1
  1.8 0.0 copy-start.2
  1.8 0.7 copy-done.2
  2.5 0.0 copy-start.3
  2.5 0.7 copy-done.3
  3.2 99.8 %sector_product.1 = bf16[8,3,128,128]{3,2,1,0:T(8,128)(2,1)S(1)} custom-call(s32[16]{0:T(128)S(1)} %copy-done.3, s32[8,16]{1,0:T(8,128)S(1)} %copy-done.1, s32[8,16]{1,0:T(8,128)S(1)} %copy-done.2, s32[8,16]{1,0:T(8,128)S(1)} %copy-done.2, bf16[8,3,128,128]{3,2,1,0:T(8,128)(2,1)S(1)} %copy-done, bf16[8,16,128,128]{3,2,1,0:T(8,128)(2,1)} %left.1, ...), custom_call_target="tpu_custom_call" | custom-call | flops 3221225472 | bytes 8388608 | tf_op jit(solution)/shard_map/sector_product/pallas_call | solution.py:200
  102.9 0.9 copy.8
Async XLA Ops:
  0.0 1.1 %copy-start = (bf16[8,3,128,128]{3,2,1,0:T(8,128)(2,1)S(1)}, bf16[8,3,128,128]{3,2,1,0:T(8,128)(2,1)}, u32[]{:S(2)}) copy-start(bf16[8,3,128,128]{3,2,1,0:T(8,128)(2,1)} %wave.1) | copy-start | bytes 2359300
  1.1 0.7 copy-start.1
  1.8 0.7 copy-start.2
  2.5 0.7 copy-start.3

commit v2 on v1

--- a/solution.py
+++ b/solution.py
@@ -26,9 +26,9 @@
 
 
 def kernel(
-    n, pieces, shifts, mask, slots, slots_v, wave, left, right, out,
-    wpad, left_v, done, recv, terms, inverse,
-    local_sem, left_sem, halo_send, halo_recv, send_sem, recv_sem,
+    n, pieces, shifts_in, mask_in, slots_in, wave, left, right, out,
+    shifts, mask, slots, slots_v, wpad, left_v, done, recv, terms, inverse,
+    local_sem, table_sem, left_sem, halo_send, halo_recv, send_sem, recv_sem,
 ):
     me = lax.axis_index("blk")
     blocks, term_count = left.shape[0], left.shape[1]
@@ -46,6 +46,14 @@
             barrier, inc=1, device_id={"blk": partner(me, k, n)}, device_id_type=MESH
         )
 
+    table_copies = [
+        pltpu.make_async_copy(source, target, table_sem.at[i])
+        for i, (source, target) in enumerate(
+            ((shifts_in, shifts), (mask_in, mask), (slots_in, slots), (slots_in, slots_v))
+        )
+    ]
+    for copy in table_copies:
+        copy.start()
     wave_copy = pltpu.make_async_copy(wave, wpad.at[pl.ds(1, blocks)], local_sem.at[0])
     wave_copy.start()
     own = pl.ds(me * per, per)
@@ -105,6 +113,9 @@
         @pl.loop(0, n - 1)
         def _(step, piece=piece):
             sending(step, piece).start()
+
+    for copy in table_copies:
+        copy.wait()
 
     table = slots_v[...]
     place = lax.broadcasted_iota(jnp.int32, table.shape, 0) * term_count + lax.broadcasted_iota(
@@ -193,16 +204,18 @@
     items = blocks * term_count
     per = items // n
     pieces = PIECES if per % PIECES == 0 else 1
-    smem = pl.BlockSpec(memory_space=pltpu.SMEM)
-    vmem = pl.BlockSpec(memory_space=pltpu.VMEM)
-    hbm = pl.BlockSpec(memory_space=pl.ANY)
+    hbm = pl.BlockSpec(memory_space=pltpu.HBM)
     dma = pltpu.SemaphoreType.DMA
     return pl.pallas_call(
         functools.partial(kernel, n, pieces),
         out_shape=jax.ShapeDtypeStruct(wavefunction.shape, jnp.bfloat16),
-        in_specs=[smem, smem, smem, vmem, hbm, hbm, hbm],
-        out_specs=vmem,
+        in_specs=[hbm] * 6,
+        out_specs=pl.BlockSpec(memory_space=pltpu.VMEM),
         scratch_shapes=[
+            pltpu.SMEM(shifts.shape, jnp.int32),
+            pltpu.SMEM(term_mask.shape, jnp.int32),
+            pltpu.SMEM(slot_table.shape, jnp.int32),
+            pltpu.VMEM(slot_table.shape, jnp.int32),
             pltpu.VMEM((blocks + 2, vectors, width, width), jnp.bfloat16),
             pltpu.VMEM((blocks, term_count, width, width), jnp.bfloat16),
             pltpu.VMEM((items, vectors * width, width), jnp.bfloat16),
@@ -210,6 +223,7 @@
             pltpu.VMEM((items, vectors * width, width), jnp.bfloat16),
             pltpu.SMEM((items,), jnp.int32),
             dma((2,)),
+            dma((4,)),
             dma((blocks,)),
             dma((2,)),
             dma((2,)),
@@ -225,7 +239,7 @@
             transcendentals=0,
         ),
         name="sector_product",
-    )(shifts, term_mask, slot_table, slot_table, wavefunction, left_operators, right_operators)
+    )(shifts, term_mask, slot_table, wavefunction, left_operators, right_operators)
 
 
 def solution(mesh):

time: 104 us -> 103 us (level)
  no operation moved by 1% of the time
where the time goes in v2:
time: 103 us
  Pallas kernels  98.8 us (96%)
  local copies, waits for them, and re-layouts  4.04 us (4%)
    pallas_call x1, Pallas kernels, per_device(): pl.pallas_call(functools.partial(kernel, n, pieces), out_shape=jax.ShapeD...  98.8 us
    unnamed x9, local copies, waits for them, and re-layouts  4.04 us

profile of v2, /device:TPU:13, one launch (start us, length us, event | category | flops | bytes accessed | tf_op | source)
XLA Modules:
  0.0 102.9 jit_solution(16952439972464249473)
XLA Ops:
  0.0 0.0 copy-start
  0.0 1.1 %copy-done = bf16[8,3,128,128]{3,2,1,0:T(8,128)(2,1)S(1)} copy-done((bf16[8,3,128,128]{3,2,1,0:T(8,128)(2,1)S(1)}, bf16[8,3,128,128]{3,2,1,0:T(8,128)(2,1)}, u32[]{:S(2)}) %copy-start) | copy-done | bytes 786456
  1.1 0.0 copy-start.1
  1.1 0.7 copy-done.1
  1.8 0.0 copy-start.2
  1.8 0.7 copy-done.2
  2.5 0.0 copy-start.3
  2.5 0.7 copy-done.3
  3.2 98.8 %sector_product.1 = bf16[8,3,128,128]{3,2,1,0:T(8,128)(2,1)S(1)} custom-call(s32[16]{0:T(128)S(1)} %copy-done.3, s32[8,16]{1,0:T(8,128)S(1)} %copy-done.1, s32[8,16]{1,0:T(8,128)S(1)} %copy-done.2, bf16[8,3,128,128]{3,2,1,0:T(8,128)(2,1)S(1)} %copy-done, bf16[8,16,128,128]{3,2,1,0:T(8,128)(2,1)} %left.1, bf16[128,128,128]{2,1,0:T(8,128)(2,1)} %right.1), custom_call_target="tpu_custom_call" | custom-call | flops 3221225472 | bytes 8388608 | tf_op jit(solution)/shard_map/sector_product/pallas_call | solution.py:209
  102.0 0.9 copy.8
Async XLA Ops:
  0.0 1.1 %copy-start = (bf16[8,3,128,128]{3,2,1,0:T(8,128)(2,1)S(1)}, bf16[8,3,128,128]{3,2,1,0:T(8,128)(2,1)}, u32[]{:S(2)}) copy-start(bf16[8,3,128,128]{3,2,1,0:T(8,128)(2,1)} %wave.1) | copy-start | bytes 2359300
  1.1 0.7 copy-start.1
  1.8 0.7 copy-start.2
  2.5 0.7 copy-start.3

commit v3 on v2

--- a/solution.py
+++ b/solution.py
@@ -8,7 +8,7 @@
 from jax.sharding import PartitionSpec as P
 
 MESH = pl.DeviceIdType.MESH
-PIECES = 1
+VMEM_LIMIT = 54 * 1024 * 1024
 
 
 def partner(me, k, n):
@@ -26,8 +26,8 @@
 
 
 def kernel(
-    n, pieces, shifts_in, mask_in, slots_in, wave, left, right, out,
-    shifts, mask, slots, slots_v, wpad, left_v, done, recv, terms, inverse,
+    n, shifts_in, mask_in, slots_in, wave, left, right, out,
+    shifts, mask, slots, slots_v, wpad, left_v, done, recv, sums, item_of, sum_before,
     local_sem, table_sem, left_sem, halo_send, halo_recv, send_sem, recv_sem,
 ):
     me = lax.axis_index("blk")
@@ -35,7 +35,6 @@
     vectors, width = wave.shape[1], wave.shape[2]
     items = blocks * term_count
     per = items // n
-    size = per // pieces
     last = n - 1
 
     barrier = pltpu.get_barrier_semaphore()
@@ -85,34 +84,32 @@
     def _():
         halo(False).start()
 
-    def sending(step, piece):
+    def sending(step):
         peer = partner(me, offset_of(step, n), n)
         return pltpu.make_async_remote_copy(
-            src_ref=right.at[pl.ds(peer * per + piece * size, size)],
-            dst_ref=recv.at[pl.ds(me * per + piece * size, size)],
-            send_sem=send_sem.at[piece, step],
-            recv_sem=recv_sem.at[piece, step],
+            src_ref=right.at[pl.ds(peer * per, per)],
+            dst_ref=recv.at[pl.ds(me * per, per)],
+            send_sem=send_sem.at[step],
+            recv_sem=recv_sem.at[step],
             device_id={"blk": peer},
             device_id_type=MESH,
         )
 
-    def arriving(step, piece):
+    def arriving(step):
         peer = partner(me, offset_of(step, n), n)
-        here = recv.at[pl.ds(peer * per + piece * size, size)]
+        here = recv.at[pl.ds(peer * per, per)]
         return pltpu.make_async_remote_copy(
             src_ref=here,
             dst_ref=here,
-            send_sem=send_sem.at[piece, step],
-            recv_sem=recv_sem.at[piece, step],
+            send_sem=send_sem.at[step],
+            recv_sem=recv_sem.at[step],
             device_id={"blk": peer},
             device_id_type=MESH,
         )
 
-    for piece in range(pieces):
-
-        @pl.loop(0, n - 1)
-        def _(step, piece=piece):
-            sending(step, piece).start()
+    @pl.loop(0, n - 1)
+    def _(step):
+        sending(step).start()
 
     for copy in table_copies:
         copy.wait()
@@ -121,10 +118,24 @@
     place = lax.broadcasted_iota(jnp.int32, table.shape, 0) * term_count + lax.broadcasted_iota(
         jnp.int32, table.shape, 1
     )
-
-    @pl.loop(0, items)
-    def _(s):
-        inverse[s] = jnp.max(jnp.where(table == s, place, 0))
+    offset = partner(me, table // per, n)
+    rank = jnp.where(
+        offset == 0, 0, jnp.where(offset >= n // 2, 2 * offset - n + 1, 2 * offset)
+    )
+    position = rank * per + table % per
+
+    def look_up(p, latest):
+        here = position == p
+        row = jnp.max(here.astype(jnp.int32), axis=1, keepdims=True)
+        item_of[p] = jnp.max(jnp.where(here, place, 0))
+        sum_before[p] = jnp.max(row * latest)
+        return jnp.where(row > 0, p + 1, latest)
+
+    latest = lax.fori_loop(0, items, look_up, jnp.zeros((blocks, 1), jnp.int32))
+    rows = lax.broadcasted_iota(jnp.int32, (blocks, 1), 0)
+    for a in range(blocks):
+        sum_before[items + a] = jnp.max(jnp.where(rows == a, latest, 0))
+    sums[0] = jnp.zeros(sums.shape[1:], sums.dtype)
 
     wave_copy.wait()
 
@@ -163,38 +174,32 @@
                     :, v * width : (v + 1) * width
                 ]
 
-    def multiply(first, count):
-        for j in range(count):
-            s = first + j
-            terms[s] = lax.dot_general(
-                done[inverse[s]],
-                recv[s],
+    def multiply(place, first):
+        for j in range(per):
+            term = lax.dot_general(
+                done[item_of[place + j]],
+                recv[first + j],
                 (((1,), (1,)), ((), ())),
                 preferred_element_type=jnp.float32,
             ).astype(jnp.bfloat16)
+            sums[place + j + 1] = sums[sum_before[place + j]] + term.astype(jnp.float32)
 
     own_copy.wait()
-    multiply(me * per, per)
-    for piece in range(pieces):
-
-        @pl.loop(0, n - 1)
-        def _(step, piece=piece):
-            arriving(step, piece).wait_recv()
-            multiply(partner(me, offset_of(step, n), n) * per + piece * size, size)
+    multiply(0, me * per)
+    @pl.loop(0, n - 1)
+    def _(step):
+        arriving(step).wait_recv()
+        multiply((step + 1) * per, partner(me, offset_of(step, n), n) * per)
 
     @pl.loop(0, blocks)
     def _(a):
+        total = sums[sum_before[items + a]]
         for v in range(vectors):
-            total = jnp.zeros((width, width), jnp.float32)
-            for t in range(term_count):
-                total += terms[slots[a, t], pl.ds(v * width, width)].astype(jnp.float32)
-            out[a, v] = total.astype(out.dtype)
-
-    for piece in range(pieces):
-
-        @pl.loop(0, n - 1)
-        def _(step, piece=piece):
-            sending(step, piece).wait_send()
+            out[a, v] = total[v * width : (v + 1) * width].astype(out.dtype)
+
+    @pl.loop(0, n - 1)
+    def _(step):
+        sending(step).wait_send()
 
 
 def per_device(wavefunction, left_operators, right_operators, shifts, term_mask, slot_table):
@@ -203,11 +208,10 @@
     term_count = left_operators.shape[1]
     items = blocks * term_count
     per = items // n
-    pieces = PIECES if per % PIECES == 0 else 1
     hbm = pl.BlockSpec(memory_space=pltpu.HBM)
     dma = pltpu.SemaphoreType.DMA
     return pl.pallas_call(
-        functools.partial(kernel, n, pieces),
+        functools.partial(kernel, n),
         out_shape=jax.ShapeDtypeStruct(wavefunction.shape, jnp.bfloat16),
         in_specs=[hbm] * 6,
         out_specs=pl.BlockSpec(memory_space=pltpu.VMEM),
@@ -220,18 +224,19 @@
             pltpu.VMEM((blocks, term_count, width, width), jnp.bfloat16),
             pltpu.VMEM((items, vectors * width, width), jnp.bfloat16),
             pltpu.VMEM((items, width, width), jnp.bfloat16),
-            pltpu.VMEM((items, vectors * width, width), jnp.bfloat16),
+            pltpu.VMEM((items + 1, vectors * width, width), jnp.float32),
             pltpu.SMEM((items,), jnp.int32),
+            pltpu.SMEM((items + blocks,), jnp.int32),
             dma((2,)),
             dma((4,)),
             dma((blocks,)),
             dma((2,)),
             dma((2,)),
-            dma((pieces, n - 1)),
-            dma((pieces, n - 1)),
+            dma((n - 1,)),
+            dma((n - 1,)),
         ],
         compiler_params=pltpu.CompilerParams(
-            collective_id=0, has_side_effects=True, vmem_limit_bytes=52 * 1024 * 1024
+            collective_id=0, has_side_effects=True, vmem_limit_bytes=VMEM_LIMIT
         ),
         cost_estimate=pl.CostEstimate(
             flops=4 * items * vectors * width**3,

time: 103 us -> 100 us (0.971)
  local copies, waits for them, and re-layouts: 4.04 us -> 2.09 us
    unnamed x9 -> x1, local copies, waits for them, and re-layouts: 4.04 us -> 2.09 us
where the time goes in v3:
time: 100 us
  Pallas kernels  98.2 us (98%)
  local copies, waits for them, and re-layouts  2.09 us (2%)
    pallas_call x1, Pallas kernels, per_device(): pl.pallas_call(functools.partial(kernel, n), out_shape=jax.ShapeDtypeStru...  98.2 us
    unnamed x1, local copies, waits for them, and re-layouts  2.09 us

profile of v3, /device:TPU:13, one launch (start us, length us, event | category | flops | bytes accessed | tf_op | source)
XLA Modules:
  0.0 100.3 jit_solution(5798281378617117504)
XLA Ops:
  0.0 98.2 %sector_product.1 = bf16[8,3,128,128]{3,2,1,0:T(8,128)(2,1)} custom-call(s32[16]{0:T(128)} %shifts_in.1, s32[8,16]{1,0:T(8,128)} %mask_in.1, s32[8,16]{1,0:T(8,128)} %slots_in.1, bf16[8,3,128,128]{3,2,1,0:T(8,128)(2,1)} %wave.1, bf16[8,16,128,128]{3,2,1,0:T(8,128)(2,1)} %left.1, bf16[128,128,128]{2,1,0:T(8,128)(2,1)} %right.1), custom_call_target="tpu_custom_call" | custom-call | flops 3221225472 | bytes 8388608 | tf_op jit(solution)/shard_map/sector_product/pallas_call | solution.py:213
  98.2 2.1 %copy.8 = bf16[8,3,128,128]{3,2,1,0:T(8,128)(2,1)} copy(bf16[8,3,128,128]{3,2,1,0:T(8,128)(2,1)} %sector_product.1) | data formatting | bytes 1572864

commit v4 on v3

--- a/solution.py
+++ b/solution.py
@@ -8,7 +8,7 @@
 from jax.sharding import PartitionSpec as P
 
 MESH = pl.DeviceIdType.MESH
-VMEM_LIMIT = 54 * 1024 * 1024
+VMEM_LIMIT = 53 * 1024 * 1024
 
 
 def partner(me, k, n):
@@ -26,8 +26,8 @@
 
 
 def kernel(
-    n, shifts_in, mask_in, slots_in, wave, left, right, out,
-    shifts, mask, slots, slots_v, wpad, left_v, done, recv, sums, item_of, sum_before,
+    n, tables_in, wave, left, right, out,
+    tables, tables_v, wpad, left_v, done, recv, sums, item_of, sum_before,
     local_sem, table_sem, left_sem, halo_send, halo_recv, send_sem, recv_sem,
 ):
     me = lax.axis_index("blk")
@@ -48,7 +48,7 @@
     table_copies = [
         pltpu.make_async_copy(source, target, table_sem.at[i])
         for i, (source, target) in enumerate(
-            ((shifts_in, shifts), (mask_in, mask), (slots_in, slots), (slots_in, slots_v))
+            ((tables_in, tables), (tables_in, tables_v))
         )
     ]
     for copy in table_copies:
@@ -114,7 +114,7 @@
     for copy in table_copies:
         copy.wait()
 
-    table = slots_v[...]
+    table = tables_v[pl.ds(0, blocks)] // 2
     place = lax.broadcasted_iota(jnp.int32, table.shape, 0) * term_count + lax.broadcasted_iota(
         jnp.int32, table.shape, 1
     )
@@ -164,11 +164,11 @@
     def _(a):
         @pl.loop(0, term_count)
         def _(t):
-            row = a + 1 - shifts[t]
+            row = a + 1 - tables[blocks, t]
             piece = wpad[row]
             beside = jnp.concatenate([piece[v] for v in range(vectors)], axis=1)
             product = jnp.dot(left_v[a, t], beside, preferred_element_type=jnp.float32)
-            product = (product * mask[a, t].astype(jnp.float32)).astype(jnp.bfloat16)
+            product = (product * (tables[a, t] % 2).astype(jnp.float32)).astype(jnp.bfloat16)
             for v in range(vectors):
                 done[a * term_count + t, pl.ds(v * width, width)] = product[
                     :, v * width : (v + 1) * width
@@ -208,18 +208,17 @@
     term_count = left_operators.shape[1]
     items = blocks * term_count
     per = items // n
+    tables = jnp.concatenate([slot_table * 2 + term_mask, shifts[None]], axis=0)
     hbm = pl.BlockSpec(memory_space=pltpu.HBM)
     dma = pltpu.SemaphoreType.DMA
     return pl.pallas_call(
         functools.partial(kernel, n),
         out_shape=jax.ShapeDtypeStruct(wavefunction.shape, jnp.bfloat16),
-        in_specs=[hbm] * 6,
+        in_specs=[hbm] * 4,
         out_specs=pl.BlockSpec(memory_space=pltpu.VMEM),
         scratch_shapes=[
-            pltpu.SMEM(shifts.shape, jnp.int32),
-            pltpu.SMEM(term_mask.shape, jnp.int32),
-            pltpu.SMEM(slot_table.shape, jnp.int32),
-            pltpu.VMEM(slot_table.shape, jnp.int32),
+            pltpu.SMEM(tables.shape, jnp.int32),
+            pltpu.VMEM(tables.shape, jnp.int32),
             pltpu.VMEM((blocks + 2, vectors, width, width), jnp.bfloat16),
             pltpu.VMEM((blocks, term_count, width, width), jnp.bfloat16),
             pltpu.VMEM((items, vectors * width, width), jnp.bfloat16),
@@ -228,7 +227,7 @@
             pltpu.SMEM((items,), jnp.int32),
             pltpu.SMEM((items + blocks,), jnp.int32),
             dma((2,)),
-            dma((4,)),
+            dma((2,)),
             dma((blocks,)),
             dma((2,)),
             dma((2,)),
@@ -244,7 +243,7 @@
             transcendentals=0,
         ),
         name="sector_product",
-    )(shifts, term_mask, slot_table, wavefunction, left_operators, right_operators)
+    )(tables, wavefunction, left_operators, right_operators)
 
 
 def solution(mesh):

time: 100 us -> 99.8 us (level)
  other arithmetic: 0 us -> 1.37 us
  local copies, waits for them, and re-layouts: 2.09 us -> 0.88 us
    unnamed x1, local copies, waits for them, and re-layouts: 2.09 us -> 0.88 us
where the time goes in v4:
time: 99.8 us; the launch traced here: 99.6 us
  Pallas kernels  97.3 us (97%)
  other arithmetic  1.37 us (1%)
    pallas_call x1, Pallas kernels, per_device(): pl.pallas_call(functools.partial(kernel, n), out_shape=jax.ShapeDtypeStru...  97.3 us

profile of v4, /device:TPU:13, one launch (start us, length us, event | category | flops | bytes accessed | tf_op | source)
XLA Modules:
  0.0 99.6 jit_solution(14914902996101663841)
XLA Ops:
  0.0 0.7 multiply_add_fusion
  0.7 0.7 pad_add_fusion.tables_in
  1.4 97.3 %sector_product.1 = bf16[8,3,128,128]{3,2,1,0:T(8,128)(2,1)S(1)} custom-call(s32[9,16]{1,0:T(8,128)S(1)} %pad_add_fusion.tables_in, bf16[8,3,128,128]{3,2,1,0:T(8,128)(2,1)} %wave.1, bf16[8,16,128,128]{3,2,1,0:T(8,128)(2,1)} %left.1, bf16[128,128,128]{2,1,0:T(8,128)(2,1)} %right.1), custom_call_target="tpu_custom_call" | custom-call | flops 3221225472 | bytes 8388608 | tf_op jit(solution)/shard_map/sector_product/pallas_call | solution.py:214
  98.7 0.9 copy.8

commit v5 on v4

--- a/solution.py
+++ b/solution.py
@@ -61,8 +61,6 @@
     left_copies = [
         pltpu.make_async_copy(left.at[a], left_v.at[a], left_sem.at[a]) for a in range(blocks)
     ]
-    for copy in left_copies:
-        copy.start()
 
     pl.semaphore_wait(barrier, n - 1)
 
@@ -110,6 +108,9 @@
     @pl.loop(0, n - 1)
     def _(step):
         sending(step).start()
+
+    for copy in left_copies:
+        copy.start()
 
     for copy in table_copies:
         copy.wait()

time: 99.8 us -> 99.8 us (level)
  no operation moved by 1% of the time
where the time goes in v5:
time: 99.8 us; the launch traced here: 99.6 us
  Pallas kernels  97.3 us (97%)
  other arithmetic  1.37 us (1%)
    pallas_call x1, Pallas kernels, per_device(): pl.pallas_call(functools.partial(kernel, n), out_shape=jax.ShapeDtypeStru...  97.3 us

profile of v5, /device:TPU:13, one launch (start us, length us, event | category | flops | bytes accessed | tf_op | source)
XLA Modules:
  0.0 99.6 jit_solution(17324795081844138016)
XLA Ops:
  0.0 0.7 multiply_add_fusion
  0.7 0.7 pad_add_fusion.tables_in
  1.4 97.3 %sector_product.1 = bf16[8,3,128,128]{3,2,1,0:T(8,128)(2,1)S(1)} custom-call(s32[9,16]{1,0:T(8,128)S(1)} %pad_add_fusion.tables_in, bf16[8,3,128,128]{3,2,1,0:T(8,128)(2,1)} %wave.1, bf16[8,16,128,128]{3,2,1,0:T(8,128)(2,1)} %left.1, bf16[128,128,128]{2,1,0:T(8,128)(2,1)} %right.1), custom_call_target="tpu_custom_call" | custom-call | flops 3221225472 | bytes 8388608 | tf_op jit(solution)/shard_map/sector_product/pallas_call | solution.py:215
  98.7 0.9 copy.8
